TPU v7x, 32 devices: a whole 2x2x4 slice. The times are simulated.
32 devices in a mesh: arc: 8 (over y, x, core), mas: 4 (over z).
Axes of the slice: x: 2, y: 2, z: 4, core: 2. Of those that a mesh axis runs over, the one named last changes fastest.
Arguments:
- jac: bfloat16 [8, 16, 1024, 256], P('arc', 'mas')
- resid: float32 [8, 1024], P('arc'), may hold values from -6 to 6
- counts: int32 [8], P('arc'), may hold values from 512 to 1024
- vis: int32 [8, 16], P('arc'), may hold values from 0 to 39, as said below
- xcur: float32 [40, 256], P('mas'), may hold values from -6 to 6
- damp: float32 [40, 256], P('mas'), may hold values from 2 to 20
Outputs:
- updated: float32 [40, 256], P('mas')
- postfit: float32 [8, 1024], P('arc', 'mas')
Inputs may be any that keep to these rules, and one draw needn't show every extreme that they name: `vis`: each row names 16 distinct blocks; block b is held by index b // 10 of mas.
All inputs are finite; a program needn't handle non-finite values.
Results may differ from a plain program's by a relative error of at most 0.0003.
Values sent between devices are 32-bit elements; how exact they have to be, the bound alone decides.
A program may use at most 64 MiB of HBM per device.

v0:
```python
import jax
import jax.numpy as jnp
from jax import lax
from jax.sharding import PartitionSpec as P

ITERS = 4


def per_device(jac, resid, counts, vis, xcur, damp):
    mas_count = lax.axis_size("mas")
    mas_pos = lax.axis_index("mas")
    block_count = xcur.shape[0]
    slot_count = jac.shape[1]
    row_count = jac.shape[2]
    partials = jac[0]
    listed = vis[0]
    my_blocks = lax.dynamic_slice_in_dim(listed, mas_pos * slot_count, slot_count)
    valid_rows = jnp.arange(row_count) < counts[0]
    prefit = jnp.where(valid_rows, resid[0], 0.0)

    def spread(slot_terms):
        onehot = (my_blocks[:, None] == jnp.arange(block_count * mas_count)[None, :]).astype(
            jnp.float32
        )
        dense_sum = jnp.einsum("vn,vm->nm", onehot, slot_terms, precision=lax.Precision.HIGHEST)
        partial_sum = lax.psum_scatter(dense_sum, "mas", scatter_dimension=0, tiled=True)
        return lax.psum(partial_sum, "arc")

    def fetch(vector):
        gathered = lax.all_gather(vector, "mas", axis=0, tiled=True)
        return jnp.take(gathered, my_blocks, axis=0)

    def forward(slot_values):
        return jnp.einsum("vrm,vm->r", partials, slot_values, precision=lax.Precision.HIGHEST)

    def backward(row_values):
        return jnp.einsum("vrm,r->vm", partials, row_values, precision=lax.Precision.HIGHEST)

    def squares(remain):
        return lax.psum(jnp.sum(remain * remain), "mas")

    rhs = spread(backward(prefit))
    delta = jnp.zeros_like(rhs)
    remain = rhs
    direction = rhs
    norm_now = squares(remain)
    row_share = row_count // mas_count
    for iteration in range(ITERS):
        image_part = forward(fetch(direction))
        image_rows = jnp.where(valid_rows, lax.psum(image_part, "mas"), 0.0)
        applied = spread(backward(image_rows)) + damp * direction
        curvature = lax.psum(jnp.sum(direction * applied), "mas")
        step_len = norm_now / curvature
        delta = delta + step_len * direction
        remain = remain - step_len * applied
        norm_next = squares(remain)
        direction = remain + norm_next / norm_now * direction
        norm_now = norm_next
    change = forward(fetch(delta))
    post_sum = lax.psum_scatter(change[None, :], "mas", scatter_dimension=1, tiled=True)
    prefit_share = lax.dynamic_slice_in_dim(prefit, mas_pos * row_share, row_share)
    valid_share = lax.dynamic_slice_in_dim(valid_rows, mas_pos * row_share, row_share)
    postfit = jnp.where(valid_share, prefit_share - post_sum[0], 0.0)
    return (xcur + delta, postfit[None, :])


def solution(mesh):
    return jax.shard_map(
        per_device,
        mesh=mesh,
        in_specs=(
            P("arc", "mas", None, None),
            P("arc", None),
            P("arc"),
            P("arc", None),
            P("mas", None),
            P("mas", None),
        ),
        out_specs=(P("mas", None), P("arc", "mas")),
        check_vma=False,
    )
```

profile of v0, /device:TPU:0, one launch (start us, length us, event | category | flops | bytes accessed | tf_op | source)
XLA Modules:
  0.0 446.2 jit_solution(12359702845204120861)
XLA Ops:
  8.0 0.7 compare_and_fusion
  8.8 1.6 fusion.18
  10.4 0.3 fusion.33
  10.7 21.2 %all-reduce = f32[40,256]{1,0:T(8,128)S(1)} all-reduce(f32[40,256]{1,0:T(8,128)S(1)} %fusion.33), channel_id=2, replica_groups=mesh['arc'=8,'mas'=4] {'mas'}, use_global_device_ids=true, to_apply=%region_0.1.clone | all-reduce | flops 10240 | bytes 81920
  31.9 0.6 dynamic-slice.1
  33.2 22.3 %psum.119 = f32[10,256]{1,0:T(8,128)S(1)} all-reduce(f32[10,256]{1,0:T(8,128)S(1)} %constant_dynamic-slice_fusion.4), channel_id=1, replica_groups=mesh['arc'=8,'mas'=4] {'arc'}, use_global_device_ids=true, to_apply=%region_1.2 | all-reduce | flops 2560 | bytes 20480 | tf_op jit(solution)/shard_map/psum | solution.py:27
  55.5 13.1 %all-gather = f32[4,10,256]{2,1,0:T(8,128)S(1)} all-gather(f32[1,10,256]{2,1,0:T(8,128)S(1)} %bitcast.95), channel_id=1, replica_groups=mesh['arc'=8,'mas'=4] {'mas'}, dimensions={0}, use_global_device_ids=true | all-gather | bytes 51200 | tf_op jit(solution)/shard_map/all_gather | solution.py:30
  68.7 0.6 gather_fusion
  69.2 0.1 select_bitcast_fusion.4
  69.3 1.7 fusion.16
  71.0 8.5 %psum.121 = f32[1024]{0:T(1024)S(1)} all-reduce(f32[1024]{0:T(1024)S(1)} %bitcast.100), channel_id=1, replica_groups=mesh['arc'=8,'mas'=4] {'mas'}, use_global_device_ids=true, to_apply=%region_4.6 | all-reduce | flops 1024 | bytes 8192 | tf_op jit(solution)/shard_map/psum | solution.py:50
  79.5 0.9 fusion.14
  80.4 0.3 fusion.31
  80.7 17.9 %all-reduce.1 = f32[40,256]{1,0:T(8,128)S(1)} all-reduce(f32[40,256]{1,0:T(8,128)S(1)} %fusion.31), channel_id=3, replica_groups=mesh['arc'=8,'mas'=4] {'mas'}, use_global_device_ids=true, to_apply=%region_5.7.clone | all-reduce | flops 10240 | bytes 81920
  98.7 22.3 %psum.122 = f32[10,256]{1,0:T(8,128)S(1)} all-reduce(f32[10,256]{1,0:T(8,128)S(1)} %constant_dynamic-slice_fusion.3), channel_id=1, replica_groups=mesh['arc'=8,'mas'=4] {'arc'}, use_global_device_ids=true, to_apply=%region_6.8 | all-reduce | flops 2560 | bytes 20480 | tf_op jit(solution)/shard_map/psum | solution.py:27
  121.0 0.7 multiply_reduce_fusion.6
  121.7 9.1 %all-reduce.5 = (f32[]{:T(128)}, f32[]{:T(128)}) all-reduce(f32[]{:T(128)} %get-tuple-element.4, f32[]{:T(128)} %get-tuple-element.3), channel_id=1, replica_groups=mesh['arc'=8,'mas'=4] {'mas'}, use_global_device_ids=true, to_apply=%region_3.4 | all-reduce | flops 2 | bytes 16 | tf_op jit(solution)/shard_map/psum | solution.py:40
  132.0 0.6 multiply_reduce_fusion.5
  132.6 10.9 %psum.124 = f32[]{:T(128)} all-reduce(f32[]{:T(128)} %get-tuple-element.13), channel_id=1, replica_groups=mesh['arc'=8,'mas'=4] {'mas'}, use_global_device_ids=true, to_apply=%region_10.12 | all-reduce | flops 1 | bytes 8 | tf_op jit(solution)/shard_map/psum | solution.py:40
  144.8 13.2 %all-gather.1 = f32[4,10,256]{2,1,0:T(8,128)S(1)} all-gather(f32[1,10,256]{2,1,0:T(8,128)S(1)} %fusion.59), channel_id=1, replica_groups=mesh['arc'=8,'mas'=4] {'mas'}, dimensions={0}, use_global_device_ids=true | all-gather | bytes 51200 | tf_op jit(solution)/shard_map/all_gather | solution.py:30
  157.9 0.6 gather_fusion.1
  158.5 0.1 select_bitcast_fusion.3
  158.6 1.7 fusion.12
  160.3 8.4 %psum.125 = f32[1024]{0:T(1024)S(1)} all-reduce(f32[1024]{0:T(1024)S(1)} %bitcast.102), channel_id=1, replica_groups=mesh['arc'=8,'mas'=4] {'mas'}, use_global_device_ids=true, to_apply=%region_11.13 | all-reduce | flops 1024 | bytes 8192 | tf_op jit(solution)/shard_map/psum | solution.py:50
  168.7 0.9 fusion.10
  169.7 0.3 fusion.29
  170.0 18.0 %all-reduce.2 = f32[40,256]{1,0:T(8,128)S(1)} all-reduce(f32[40,256]{1,0:T(8,128)S(1)} %fusion.29), channel_id=4, replica_groups=mesh['arc'=8,'mas'=4] {'mas'}, use_global_device_ids=true, to_apply=%region_12.14.clone | all-reduce | flops 10240 | bytes 81920
  188.0 22.3 %psum.126 = f32[10,256]{1,0:T(8,128)S(1)} all-reduce(f32[10,256]{1,0:T(8,128)S(1)} %constant_dynamic-slice_fusion.2), channel_id=1, replica_groups=mesh['arc'=8,'mas'=4] {'arc'}, use_global_device_ids=true, to_apply=%region_13.15 | all-reduce | flops 2560 | bytes 20480 | tf_op jit(solution)/shard_map/psum | solution.py:27
  210.3 0.7 multiply_reduce_fusion.4
  211.0 9.1 %psum.127 = f32[]{:T(128)} all-reduce(f32[]{:T(128)} %multiply_reduce_fusion.4), channel_id=1, replica_groups=mesh['arc'=8,'mas'=4] {'mas'}, use_global_device_ids=true, to_apply=%region_15.17 | all-reduce | flops 1 | bytes 8 | tf_op jit(solution)/shard_map/psum | solution.py:52
  221.4 0.7 multiply_reduce_fusion.3
  222.1 11.0 %psum.128 = f32[]{:T(128)} all-reduce(f32[]{:T(128)} %get-tuple-element.11), channel_id=1, replica_groups=mesh['arc'=8,'mas'=4] {'mas'}, use_global_device_ids=true, to_apply=%region_17.19 | all-reduce | flops 1 | bytes 8 | tf_op jit(solution)/shard_map/psum | solution.py:40
  234.3 13.1 %all-gather.2 = f32[4,10,256]{2,1,0:T(8,128)S(1)} all-gather(f32[1,10,256]{2,1,0:T(8,128)S(1)} %bitcast.96), channel_id=1, replica_groups=mesh['arc'=8,'mas'=4] {'mas'}, dimensions={0}, use_global_device_ids=true | all-gather | bytes 51200 | tf_op jit(solution)/shard_map/all_gather | solution.py:30
  247.5 0.6 gather_fusion.2
  248.0 0.1 select_bitcast_fusion.2
  248.1 1.7 fusion.8
  249.8 8.4 %psum.129 = f32[1024]{0:T(1024)S(1)} all-reduce(f32[1024]{0:T(1024)S(1)} %bitcast.104), channel_id=1, replica_groups=mesh['arc'=8,'mas'=4] {'mas'}, use_global_device_ids=true, to_apply=%region_18.20 | all-reduce | flops 1024 | bytes 8192 | tf_op jit(solution)/shard_map/psum | solution.py:50
  258.2 0.9 fusion.6
  259.1 0.3 fusion.27
  259.4 18.0 %all-reduce.3 = f32[40,256]{1,0:T(8,128)S(1)} all-reduce(f32[40,256]{1,0:T(8,128)S(1)} %fusion.27), channel_id=5, replica_groups=mesh['arc'=8,'mas'=4] {'mas'}, use_global_device_ids=true, to_apply=%region_19.21.clone | all-reduce | flops 10240 | bytes 81920
  277.5 22.4 %psum.130 = f32[10,256]{1,0:T(8,128)S(1)} all-reduce(f32[10,256]{1,0:T(8,128)S(1)} %constant_dynamic-slice_fusion.1), channel_id=1, replica_groups=mesh['arc'=8,'mas'=4] {'arc'}, use_global_device_ids=true, to_apply=%region_20.22 | all-reduce | flops 2560 | bytes 20480 | tf_op jit(solution)/shard_map/psum | solution.py:27
  299.8 0.6 multiply_reduce_fusion.2
  300.4 9.0 %psum.131 = f32[]{:T(128)} all-reduce(f32[]{:T(128)} %multiply_reduce_fusion.2), channel_id=1, replica_groups=mesh['arc'=8,'mas'=4] {'mas'}, use_global_device_ids=true, to_apply=%region_22.24 | all-reduce | flops 1 | bytes 8 | tf_op jit(solution)/shard_map/psum | solution.py:52
  310.7 0.6 multiply_reduce_fusion.1
  311.3 11.0 %psum.132 = f32[]{:T(128)} all-reduce(f32[]{:T(128)} %get-tuple-element.9), channel_id=1, replica_groups=mesh['arc'=8,'mas'=4] {'mas'}, use_global_device_ids=true, to_apply=%region_24.26 | all-reduce | flops 1 | bytes 8 | tf_op jit(solution)/shard_map/psum | solution.py:40
  323.5 13.1 %all-gather.3 = f32[4,10,256]{2,1,0:T(8,128)S(1)} all-gather(f32[1,10,256]{2,1,0:T(8,128)S(1)} %fusion.51), channel_id=1, replica_groups=mesh['arc'=8,'mas'=4] {'mas'}, dimensions={0}, use_global_device_ids=true | all-gather | bytes 51200 | tf_op jit(solution)/shard_map/all_gather | solution.py:30
  336.6 0.6 gather_fusion.3
  337.2 0.1 select_bitcast_fusion.1
  337.3 1.7 fusion.4
  339.0 8.4 %psum.133 = f32[1024]{0:T(1024)S(1)} all-reduce(f32[1024]{0:T(1024)S(1)} %bitcast.106), channel_id=1, replica_groups=mesh['arc'=8,'mas'=4] {'mas'}, use_global_device_ids=true, to_apply=%region_25.27 | all-reduce | flops 1024 | bytes 8192 | tf_op jit(solution)/shard_map/psum | solution.py:50
  347.4 0.9 fusion.2
  348.3 0.3 fusion.25
  348.6 18.0 %all-reduce.4 = f32[40,256]{1,0:T(8,128)S(1)} all-reduce(f32[40,256]{1,0:T(8,128)S(1)} %fusion.25), channel_id=6, replica_groups=mesh['arc'=8,'mas'=4] {'mas'}, use_global_device_ids=true, to_apply=%region_26.28.clone | all-reduce | flops 10240 | bytes 81920
  366.7 22.3 %psum.134 = f32[10,256]{1,0:T(8,128)S(1)} all-reduce(f32[10,256]{1,0:T(8,128)S(1)} %constant_dynamic-slice_fusion), channel_id=1, replica_groups=mesh['arc'=8,'mas'=4] {'arc'}, use_global_device_ids=true, to_apply=%region_27.29 | all-reduce | flops 2560 | bytes 20480 | tf_op jit(solution)/shard_map/psum | solution.py:27
  389.0 0.7 multiply_reduce_fusion
  389.7 9.1 %psum.135 = f32[]{:T(128)} all-reduce(f32[]{:T(128)} %multiply_reduce_fusion), channel_id=1, replica_groups=mesh['arc'=8,'mas'=4] {'mas'}, use_global_device_ids=true, to_apply=%region_29.31 | all-reduce | flops 1 | bytes 8 | tf_op jit(solution)/shard_map/psum | solution.py:52
  400.1 0.6 fusion.61
  400.7 13.1 %all-gather.4 = f32[4,10,256]{2,1,0:T(8,128)S(1)} all-gather(f32[1,10,256]{2,1,0:T(8,128)S(1)} %bitcast.98), channel_id=1, replica_groups=mesh['arc'=8,'mas'=4] {'mas'}, dimensions={0}, use_global_device_ids=true | all-gather | bytes 51200 | tf_op jit(solution)/shard_map/all_gather | solution.py:30
  413.9 0.6 gather_fusion.4
  414.4 0.1 select_bitcast_fusion
  414.5 2.5 fusion.20
  417.1 20.6 %reduce-scatter.4.cloned.1.call-done = f32[256,1]{1,0:T(8,128)} async-done(((f32[1024,1]{1,0:T(8,128)}), f32[256,1]{1,0:T(8,128)}) %reduce-scatter.4.cloned.1.call-update) | async-done | bytes 1040
  437.7 1.0 copy.19
  438.7 0.7 dynamic-slice_select_fusion
  (33 shorter events, 0.2 us)
Async XLA Ops:
  7.2 1.6 copy-start
  7.2 24.7 %copy-start.4 = (u32[32]{0:T(128)S(1)}, u32[32]{0:T(128)}, u32[]{:S(2)}) copy-start(u32[32]{0:T(128)} %constant.35) | copy-start | bytes 388
  7.2 430.5 %reduce-scatter.4.cloned.1.call-start = ((), (), s32[]{:S(2)}) async-start(), calls=%async_computation.1 | async-start | bytes 655360
  69.3 51.7 %copy-start.1 = (f32[10,256]{1,0:T(8,128)S(1)}, f32[10,256]{1,0:T(8,128)}, u32[]{:S(2)}) copy-start(f32[10,256]{1,0:T(8,128)} %param.13) | copy-start | bytes 30724
  337.3 62.8 %copy-start.3 = (f32[10,256]{1,0:T(8,128)S(1)}, f32[10,256]{1,0:T(8,128)}, u32[]{:S(2)}) copy-start(f32[10,256]{1,0:T(8,128)} %param.12) | copy-start | bytes 30724
  348.3 68.8 %copy-start.2 = (f32[1,1024]{1,0:T(1,128)S(1)}, f32[1,1024]{1,0:T(1,128)}, u32[]{:S(2)}) copy-start(f32[1,1024]{1,0:T(1,128)} %param.9) | copy-start | bytes 12292
Sparse Core Ops, SparseCore 0:
  417.2 20.4 reduce-scatter.3
where the time goes:
time: 447 us; the launch traced here: 446 us
  blocking collectives  373 us (83%)
  between operations  24.7 us (6%)
  waiting for transfers between devices  20.6 us (5%)
  matrix products  16.1 us (4%)
  other arithmetic  7.02 us (2%)
  local copies, waits for them, and re-layouts  4.5 us (1%)
    psum x5, blocking collectives, spread(): return lax.psum(partial_sum, 'arc')  112 us
    unnamed x5, blocking collectives  93.2 us
    all_gather x5, blocking collectives, fetch(): gathered = lax.all_gather(vector, 'mas', axis=0, tiled=True)  65.7 us
    psum x4, blocking collectives, squares(): return lax.psum(jnp.sum(remain * remain), 'mas')  41.9 us
    psum x4, blocking collectives, per_device(): image_rows = jnp.where(valid_rows, lax.psum(image_part, 'mas'), 0.0)  33.7 us
    psum x3, blocking collectives, per_device(): curvature = lax.psum(jnp.sum(direction * applied), 'mas')  27.1 us
    unnamed x2, waiting for transfers between devices  20.6 us
    dot_general x5, matrix products, forward(): jnp.einsum('vrm,vm->r', partials, slot_values, precision=lax.Precision.HI...  9.41 us
  transfers between devices with their start and end apart: 1, of which 1 were waited for; matrix products, arithmetic and copies ran while one was open for 0% of the time, Pallas kernels for 0%

commit v1 on v0

--- a/solution.py
+++ b/solution.py
@@ -24,7 +24,7 @@
         )
         dense_sum = jnp.einsum("vn,vm->nm", onehot, slot_terms, precision=lax.Precision.HIGHEST)
         partial_sum = lax.psum_scatter(dense_sum, "mas", scatter_dimension=0, tiled=True)
-        return lax.psum(partial_sum, "arc")
+        return jnp.sum(lax.all_gather(partial_sum, "arc"), axis=0)
 
     def fetch(vector):
         gathered = lax.all_gather(vector, "mas", axis=0, tiled=True)

time: 447 us -> 380 us (0.85)
  blocking collectives: 373 us -> 306 us
    psum x5 -> x0, blocking collectives: 112 us -> none  [spread(): return lax.psum(partial_sum, 'arc')]
    all_gather x0 -> x5, blocking collectives: none -> 44.1 us  [spread(): return jnp.sum(lax.all_gather(partial_sum, 'arc'), axis=0)]
where the time goes in v1:
time: 380 us; the launch traced here: 379 us
  blocking collectives  306 us (81%)
  between operations  24.7 us (6%)
  waiting for transfers between devices  20.3 us (5%)
  matrix products  16.2 us (4%)
  other arithmetic  7.1 us (2%)
  local copies, waits for them, and re-layouts  4.5 us (1%)
    unnamed x5, blocking collectives  92.6 us
    all_gather x5, blocking collectives, fetch(): gathered = lax.all_gather(vector, 'mas', axis=0, tiled=True)  65.9 us
    all_gather x5, blocking collectives, spread(): return jnp.sum(lax.all_gather(partial_sum, 'arc'), axis=0)  44.1 us
    psum x4, blocking collectives, squares(): return lax.psum(jnp.sum(remain * remain), 'mas')  41.5 us
    psum x4, blocking collectives, per_device(): image_rows = jnp.where(valid_rows, lax.psum(image_part, 'mas'), 0.0)  34.3 us
    psum x3, blocking collectives, per_device(): curvature = lax.psum(jnp.sum(direction * applied), 'mas')  27.6 us
    unnamed x2, waiting for transfers between devices  20.3 us
    dot_general x5, matrix products, forward(): jnp.einsum('vrm,vm->r', partials, slot_values, precision=lax.Precision.HI...  9.41 us
  transfers between devices with their start and end apart: 1, of which 1 were waited for; matrix products, arithmetic and copies ran while one was open for 0% of the time, Pallas kernels for 0%

profile of v1, /device:TPU:0, one launch (start us, length us, event | category | flops | bytes accessed | tf_op | source)
XLA Modules:
  0.0 378.8 jit_solution(11289251422591067651)
XLA Ops:
  8.0 0.7 compare_and_fusion
  8.8 1.6 fusion.18
  10.4 0.3 fusion.33
  10.7 21.2 %all-reduce = f32[40,256]{1,0:T(8,128)S(1)} all-reduce(f32[40,256]{1,0:T(8,128)S(1)} %fusion.33), channel_id=7, replica_groups=mesh['arc'=8,'mas'=4] {'mas'}, use_global_device_ids=true, to_apply=%region_0.1.clone | all-reduce | flops 10240 | bytes 81920
  31.9 0.6 dynamic-slice.1
  33.2 9.2 %all-gather.5 = f32[8,10,256]{2,1,0:T(8,128)S(1)} all-gather(f32[1,10,256]{2,1,0:T(8,128)S(1)} %dynamic-slice_bitcast_fusion.4), channel_id=2, replica_groups=mesh['arc'=8,'mas'=4] {'arc'}, dimensions={0}, use_global_device_ids=true | all-gather | bytes 92160 | tf_op jit(solution)/shard_map/all_gather | solution.py:27
  42.4 13.1 %all-gather.6 = f32[4,10,256]{2,1,0:T(8,128)S(1)} all-gather(f32[1,10,256]{2,1,0:T(8,128)S(1)} %bitcast.105), channel_id=1, replica_groups=mesh['arc'=8,'mas'=4] {'mas'}, dimensions={0}, use_global_device_ids=true | all-gather | bytes 51200 | tf_op jit(solution)/shard_map/all_gather | solution.py:30
  55.6 0.6 gather_fusion
  56.1 0.1 select_bitcast_fusion.4
  56.2 1.7 fusion.16
  57.9 8.4 %psum.85 = f32[1024]{0:T(1024)S(1)} all-reduce(f32[1024]{0:T(1024)S(1)} %bitcast.110), channel_id=1, replica_groups=mesh['arc'=8,'mas'=4] {'mas'}, use_global_device_ids=true, to_apply=%region_4.6 | all-reduce | flops 1024 | bytes 8192 | tf_op jit(solution)/shard_map/psum | solution.py:50
  66.4 0.9 fusion.14
  67.3 0.3 fusion.31
  67.6 18.0 %all-reduce.1 = f32[40,256]{1,0:T(8,128)S(1)} all-reduce(f32[40,256]{1,0:T(8,128)S(1)} %fusion.31), channel_id=8, replica_groups=mesh['arc'=8,'mas'=4] {'mas'}, use_global_device_ids=true, to_apply=%region_5.7.clone | all-reduce | flops 10240 | bytes 81920
  85.6 9.2 %all-gather.7 = f32[8,10,256]{2,1,0:T(8,128)S(1)} all-gather(f32[1,10,256]{2,1,0:T(8,128)S(1)} %dynamic-slice_bitcast_fusion.3), channel_id=3, replica_groups=mesh['arc'=8,'mas'=4] {'arc'}, dimensions={0}, use_global_device_ids=true | all-gather | bytes 92160 | tf_op jit(solution)/shard_map/all_gather | solution.py:27
  94.8 0.7 multiply_reduce_fusion.6
  95.5 9.0 %all-reduce.5 = (f32[]{:T(128)}, f32[]{:T(128)}) all-reduce(f32[]{:T(128)} %get-tuple-element.4, f32[]{:T(128)} %get-tuple-element.3), channel_id=1, replica_groups=mesh['arc'=8,'mas'=4] {'mas'}, use_global_device_ids=true, to_apply=%region_3.4 | all-reduce | flops 2 | bytes 16 | tf_op jit(solution)/shard_map/psum | solution.py:40
  105.7 0.6 multiply_reduce_fusion.5
  106.3 11.0 %psum.87 = f32[]{:T(128)} all-reduce(f32[]{:T(128)} %get-tuple-element.13), channel_id=1, replica_groups=mesh['arc'=8,'mas'=4] {'mas'}, use_global_device_ids=true, to_apply=%region_10.12 | all-reduce | flops 1 | bytes 8 | tf_op jit(solution)/shard_map/psum | solution.py:40
  118.6 13.1 %all-gather.8 = f32[4,10,256]{2,1,0:T(8,128)S(1)} all-gather(f32[1,10,256]{2,1,0:T(8,128)S(1)} %fusion.59), channel_id=1, replica_groups=mesh['arc'=8,'mas'=4] {'mas'}, dimensions={0}, use_global_device_ids=true | all-gather | bytes 51200 | tf_op jit(solution)/shard_map/all_gather | solution.py:30
  131.7 0.6 gather_fusion.1
  132.3 0.1 select_bitcast_fusion.3
  132.4 1.7 fusion.12
  134.1 8.5 %psum.88 = f32[1024]{0:T(1024)S(1)} all-reduce(f32[1024]{0:T(1024)S(1)} %bitcast.112), channel_id=1, replica_groups=mesh['arc'=8,'mas'=4] {'mas'}, use_global_device_ids=true, to_apply=%region_11.13 | all-reduce | flops 1024 | bytes 8192 | tf_op jit(solution)/shard_map/psum | solution.py:50
  142.6 0.9 fusion.10
  143.5 0.3 fusion.29
  143.8 17.9 %all-reduce.2 = f32[40,256]{1,0:T(8,128)S(1)} all-reduce(f32[40,256]{1,0:T(8,128)S(1)} %fusion.29), channel_id=9, replica_groups=mesh['arc'=8,'mas'=4] {'mas'}, use_global_device_ids=true, to_apply=%region_12.14.clone | all-reduce | flops 10240 | bytes 81920
  161.7 8.3 %all-gather.9 = f32[8,10,256]{2,1,0:T(8,128)S(1)} all-gather(f32[1,10,256]{2,1,0:T(8,128)S(1)} %dynamic-slice_bitcast_fusion.2), channel_id=4, replica_groups=mesh['arc'=8,'mas'=4] {'arc'}, dimensions={0}, use_global_device_ids=true | all-gather | bytes 92160 | tf_op jit(solution)/shard_map/all_gather | solution.py:27
  170.0 0.7 multiply_reduce_fusion.4
  170.7 9.2 %psum.89 = f32[]{:T(128)} all-reduce(f32[]{:T(128)} %multiply_reduce_fusion.4), channel_id=1, replica_groups=mesh['arc'=8,'mas'=4] {'mas'}, use_global_device_ids=true, to_apply=%region_15.17 | all-reduce | flops 1 | bytes 8 | tf_op jit(solution)/shard_map/psum | solution.py:52
  181.2 0.7 multiply_reduce_fusion.3
  181.9 10.9 %psum.90 = f32[]{:T(128)} all-reduce(f32[]{:T(128)} %get-tuple-element.11), channel_id=1, replica_groups=mesh['arc'=8,'mas'=4] {'mas'}, use_global_device_ids=true, to_apply=%region_17.19 | all-reduce | flops 1 | bytes 8 | tf_op jit(solution)/shard_map/psum | solution.py:40
  194.0 13.1 %all-gather.10 = f32[4,10,256]{2,1,0:T(8,128)S(1)} all-gather(f32[1,10,256]{2,1,0:T(8,128)S(1)} %bitcast.106), channel_id=1, replica_groups=mesh['arc'=8,'mas'=4] {'mas'}, dimensions={0}, use_global_device_ids=true | all-gather | bytes 51200 | tf_op jit(solution)/shard_map/all_gather | solution.py:30
  207.2 0.6 gather_fusion.2
  207.8 0.1 select_bitcast_fusion.2
  207.8 1.7 fusion.8
  209.6 8.7 %psum.91 = f32[1024]{0:T(1024)S(1)} all-reduce(f32[1024]{0:T(1024)S(1)} %bitcast.114), channel_id=1, replica_groups=mesh['arc'=8,'mas'=4] {'mas'}, use_global_device_ids=true, to_apply=%region_18.20 | all-reduce | flops 1024 | bytes 8192 | tf_op jit(solution)/shard_map/psum | solution.py:50
  218.2 0.9 fusion.6
  219.2 0.3 fusion.27
  219.5 17.7 %all-reduce.3 = f32[40,256]{1,0:T(8,128)S(1)} all-reduce(f32[40,256]{1,0:T(8,128)S(1)} %fusion.27), channel_id=10, replica_groups=mesh['arc'=8,'mas'=4] {'mas'}, use_global_device_ids=true, to_apply=%region_19.21.clone | all-reduce | flops 10240 | bytes 81920
  237.2 9.2 %all-gather.11 = f32[8,10,256]{2,1,0:T(8,128)S(1)} all-gather(f32[1,10,256]{2,1,0:T(8,128)S(1)} %dynamic-slice_bitcast_fusion.1), channel_id=5, replica_groups=mesh['arc'=8,'mas'=4] {'arc'}, dimensions={0}, use_global_device_ids=true | all-gather | bytes 92160 | tf_op jit(solution)/shard_map/all_gather | solution.py:27
  246.4 0.6 multiply_reduce_fusion.2
  247.0 9.2 %psum.92 = f32[]{:T(128)} all-reduce(f32[]{:T(128)} %multiply_reduce_fusion.2), channel_id=1, replica_groups=mesh['arc'=8,'mas'=4] {'mas'}, use_global_device_ids=true, to_apply=%region_22.24 | all-reduce | flops 1 | bytes 8 | tf_op jit(solution)/shard_map/psum | solution.py:52
  257.5 0.6 multiply_reduce_fusion.1
  258.1 10.7 %psum.93 = f32[]{:T(128)} all-reduce(f32[]{:T(128)} %get-tuple-element.9), channel_id=1, replica_groups=mesh['arc'=8,'mas'=4] {'mas'}, use_global_device_ids=true, to_apply=%region_24.26 | all-reduce | flops 1 | bytes 8 | tf_op jit(solution)/shard_map/psum | solution.py:40
  270.1 13.3 %all-gather.12 = f32[4,10,256]{2,1,0:T(8,128)S(1)} all-gather(f32[1,10,256]{2,1,0:T(8,128)S(1)} %fusion.51), channel_id=1, replica_groups=mesh['arc'=8,'mas'=4] {'mas'}, dimensions={0}, use_global_device_ids=true | all-gather | bytes 51200 | tf_op jit(solution)/shard_map/all_gather | solution.py:30
  283.4 0.6 gather_fusion.3
  284.0 0.1 select_bitcast_fusion.1
  284.1 1.7 fusion.4
  285.8 8.6 %psum.94 = f32[1024]{0:T(1024)S(1)} all-reduce(f32[1024]{0:T(1024)S(1)} %bitcast.116), channel_id=1, replica_groups=mesh['arc'=8,'mas'=4] {'mas'}, use_global_device_ids=true, to_apply=%region_25.27 | all-reduce | flops 1024 | bytes 8192 | tf_op jit(solution)/shard_map/psum | solution.py:50
  294.4 0.9 fusion.2
  295.3 0.3 fusion.25
  295.6 17.8 %all-reduce.4 = f32[40,256]{1,0:T(8,128)S(1)} all-reduce(f32[40,256]{1,0:T(8,128)S(1)} %fusion.25), channel_id=11, replica_groups=mesh['arc'=8,'mas'=4] {'mas'}, use_global_device_ids=true, to_apply=%region_26.28.clone | all-reduce | flops 10240 | bytes 81920
  313.5 8.3 %all-gather.13 = f32[8,10,256]{2,1,0:T(8,128)S(1)} all-gather(f32[1,10,256]{2,1,0:T(8,128)S(1)} %dynamic-slice_bitcast_fusion), channel_id=6, replica_groups=mesh['arc'=8,'mas'=4] {'arc'}, dimensions={0}, use_global_device_ids=true | all-gather | bytes 92160 | tf_op jit(solution)/shard_map/all_gather | solution.py:27
  321.7 0.7 multiply_reduce_fusion
  322.4 9.2 %psum.95 = f32[]{:T(128)} all-reduce(f32[]{:T(128)} %multiply_reduce_fusion), channel_id=1, replica_groups=mesh['arc'=8,'mas'=4] {'mas'}, use_global_device_ids=true, to_apply=%region_29.31 | all-reduce | flops 1 | bytes 8 | tf_op jit(solution)/shard_map/psum | solution.py:52
  333.0 0.6 fusion.61
  333.6 13.2 %all-gather.14 = f32[4,10,256]{2,1,0:T(8,128)S(1)} all-gather(f32[1,10,256]{2,1,0:T(8,128)S(1)} %bitcast.108), channel_id=1, replica_groups=mesh['arc'=8,'mas'=4] {'mas'}, dimensions={0}, use_global_device_ids=true | all-gather | bytes 51200 | tf_op jit(solution)/shard_map/all_gather | solution.py:30
  346.8 0.6 gather_fusion.4
  347.4 0.1 select_bitcast_fusion
  347.5 2.6 fusion.20
  350.1 20.3 %reduce-scatter.4.cloned.1.call-done = f32[256,1]{1,0:T(8,128)} async-done(((f32[1024,1]{1,0:T(8,128)}), f32[256,1]{1,0:T(8,128)}) %reduce-scatter.4.cloned.1.call-update) | async-done | bytes 1040
  370.4 1.0 copy.19
  371.3 0.7 dynamic-slice_select_fusion
  (38 shorter events, 0.3 us)
Async XLA Ops:
  7.2 1.6 copy-start
  7.2 24.7 %copy-start.4 = (u32[32]{0:T(128)S(1)}, u32[32]{0:T(128)}, u32[]{:S(2)}) copy-start(u32[32]{0:T(128)} %constant.35) | copy-start | bytes 388
  7.2 363.2 %reduce-scatter.4.cloned.1.call-start = ((), (), s32[]{:S(2)}) async-start(), calls=%async_computation.1 | async-start | bytes 655360
  56.2 38.6 %copy-start.1 = (f32[10,256]{1,0:T(8,128)S(1)}, f32[10,256]{1,0:T(8,128)}, u32[]{:S(2)}) copy-start(f32[10,256]{1,0:T(8,128)} %param.13) | copy-start | bytes 30724
  284.1 48.9 %copy-start.3 = (f32[10,256]{1,0:T(8,128)S(1)}, f32[10,256]{1,0:T(8,128)}, u32[]{:S(2)}) copy-start(f32[10,256]{1,0:T(8,128)} %param.12) | copy-start | bytes 30724
  295.3 54.7 %copy-start.2 = (f32[1,1024]{1,0:T(1,128)S(1)}, f32[1,1024]{1,0:T(1,128)}, u32[]{:S(2)}) copy-start(f32[1,1024]{1,0:T(1,128)} %param.9) | copy-start | bytes 12292
Sparse Core Ops, SparseCore 0:
  350.2 20.1 reduce-scatter.3
